TPU v7x, 32 devices: a whole 2x2x4 slice. The times are simulated.
32 devices in a mesh: patch: 8 (over y, x, core), ulysses: 4 (over z).
Axes of the slice: x: 2, y: 2, z: 4, core: 2. Of those that a mesh axis runs over, the one named last changes fastest.
Arguments:
- fresh_queries: bfloat16 [512, 2048], P(('patch', 'ulysses')), may hold values from -12 to 12
- fresh_keys: bfloat16 [512, 2048], P(('patch', 'ulysses')), may hold values from -6 to 6
- fresh_values: bfloat16 [512, 2048], P(('patch', 'ulysses')), may hold values from -6 to 6
- outdated_keys: bfloat16 [512, 2048], P(None, 'ulysses'), may hold values from -6 to 6
- stale_values: bfloat16 [512, 2048], P(None, 'ulysses'), may hold values from -6 to 6
- key_codes: int32 [512, 2048], P('patch', 'ulysses'), may hold values from -127 to 127
- value_codes: int32 [512, 2048], P('patch', 'ulysses'), may hold values from -127 to 127
- key_code_scales: bfloat16 [64, 16], P('patch', 'ulysses'), may hold values from 0.0039978027 to 0.015991211
- value_scales: bfloat16 [64, 16], P('patch', 'ulysses'), may hold values from 0.0039978027 to 0.015991211
- out_weight: bfloat16 [2048, 3072], P('ulysses', 'patch'), may hold values from -1.5 to 1.5
Outputs:
- projected: bfloat16 [512, 3072], P(('patch', 'ulysses'))
All inputs are finite; a program needn't handle non-finite values.
Results may differ from a plain program's by a relative error of at most 0.012.
The roundings to bfloat16 on the way count: a program that leaves them out, or rounds other values in their place, can miss the bound.
Values may be sent and summed in bfloat16 or wider, within the bound.
A program may use at most 64 MiB of HBM per device.

v0:
```python
import math

import jax
import jax.numpy as jnp
from jax import lax
from jax.sharding import PartitionSpec as P

HEAD_DIM = 128
BLOCK = 8


def refresh_tile(stale_rows, code_block, scales):
    block_count = code_block.shape[0]
    local_heads = scales.shape[1]
    shaped = stale_rows.reshape(block_count, BLOCK, local_heads, HEAD_DIM).astype(jnp.float32)
    codes_wide = code_block.reshape(block_count, BLOCK, local_heads, HEAD_DIM).astype(jnp.float32)
    result = shaped + scales.astype(jnp.float32)[:, None, :, None] * codes_wide
    return result.astype(jnp.bfloat16).reshape(block_count * BLOCK, local_heads, HEAD_DIM)


def absorb_tile(state_now, query_heads, key_tile, value_tile):
    scale_qk = 1.0 / math.sqrt(HEAD_DIM)
    scores = (
        jnp.einsum("qhd,khd->hqk", query_heads, key_tile, preferred_element_type=jnp.float32)
        * scale_qk
    )
    row_max, row_sum, row_acc = state_now
    next_max = jnp.maximum(row_max, jnp.max(scores, axis=2))
    weights = jnp.exp(scores - next_max[:, :, None])
    row_sum = jnp.sum(weights, axis=2)
    weighted = jnp.einsum(
        "hqk,khd->hqd", weights.astype(jnp.bfloat16), value_tile, preferred_element_type=jnp.float32
    )
    row_acc = weighted
    return (next_max, row_sum, row_acc)


def on_device(
    fresh_queries,
    fresh_keys,
    fresh_values,
    outdated_keys,
    stale_values,
    key_codes,
    value_codes,
    key_code_scales,
    value_scales,
    out_weight,
):
    own_patch = lax.axis_index("patch")
    query_cols, key_cols, value_cols = (
        lax.all_to_all(fresh_queries, "ulysses", split_axis=1, concat_axis=0, tiled=True),
        lax.all_to_all(fresh_keys, "ulysses", split_axis=1, concat_axis=0, tiled=True),
        lax.all_to_all(fresh_values, "ulysses", split_axis=1, concat_axis=0, tiled=True),
    )
    q_rows = query_cols.shape[0]
    local_heads = query_cols.shape[1] // HEAD_DIM
    query_heads = query_cols.reshape(q_rows, local_heads, HEAD_DIM)
    key_heads = key_cols.reshape(q_rows, local_heads, HEAD_DIM)
    value_heads = value_cols.reshape(q_rows, local_heads, HEAD_DIM)
    width = local_heads * HEAD_DIM
    key_block = key_codes.astype(jnp.bfloat16).reshape(q_rows // BLOCK, BLOCK, width)
    value_block = value_codes.astype(jnp.bfloat16).reshape(q_rows // BLOCK, BLOCK, width)
    initial = (
        jnp.full((local_heads, q_rows), -1e30, jnp.float32),
        jnp.zeros((local_heads, q_rows), jnp.float32),
        jnp.zeros((local_heads, q_rows, HEAD_DIM), jnp.float32),
    )
    segment_keys = lax.all_gather(key_block, "patch", axis=0, tiled=True)
    piece_values = lax.all_gather(value_block, "patch", axis=0, tiled=True)
    segment_key_scale = lax.all_gather(key_code_scales, "patch", axis=0, tiled=True)
    piece_vscale = lax.all_gather(value_scales, "patch", axis=0, tiled=True)
    count_of_rows = segment_keys.shape[0] * BLOCK
    seen_keys = refresh_tile(outdated_keys, segment_keys, segment_key_scale)
    seen_values = refresh_tile(stale_values, piece_values, piece_vscale)
    shard_count = count_of_rows // q_rows
    shard_ids = jnp.arange(shard_count)
    is_own = jnp.repeat(shard_ids == own_patch, q_rows)
    applied_keys = jnp.where(
        is_own[:, None, None], jnp.tile(key_heads, (shard_count, 1, 1)), seen_keys
    )
    used_values = jnp.where(
        is_own[:, None, None], jnp.tile(value_heads, (shard_count, 1, 1)), seen_values
    )
    row_max, row_sum, row_acc = absorb_tile(initial, query_heads, applied_keys, used_values)
    attended = (row_acc / row_sum[:, :, None]).astype(jnp.bfloat16)
    weight_full = lax.all_gather(out_weight, "patch", axis=1, tiled=True)
    weight_heads = weight_full.reshape(local_heads, HEAD_DIM, weight_full.shape[1])
    return lax.psum_scatter(
        jnp.einsum(
            "hqd,hdc->qc", attended, weight_heads, preferred_element_type=jnp.float32
        ).astype(jnp.bfloat16),
        "ulysses",
        scatter_dimension=0,
        tiled=True,
    )


def solution(mesh):
    return jax.shard_map(
        on_device,
        mesh=mesh,
        in_specs=(
            P(("patch", "ulysses"), None),
            P(("patch", "ulysses"), None),
            P(("patch", "ulysses"), None),
            P(None, "ulysses"),
            P(None, "ulysses"),
            P("patch", "ulysses"),
            P("patch", "ulysses"),
            P("patch", "ulysses"),
            P("patch", "ulysses"),
            P("ulysses", "patch"),
        ),
        out_specs=P(("patch", "ulysses"), None),
        check_vma=False,
    )
```

profile of v0, /device:TPU:0, one launch (start us, length us, event | category | flops | bytes accessed | tf_op | source)
XLA Modules:
  0.0 113.0 jit_solution(8240799259161332170)
XLA Ops:
  6.5 0.7 all-gather.4.cloned.1.call-update
  7.3 1.5 %copy.69 = bf16[2,4,8,512]{3,2,0,1:T(8,128)(2,1)} copy(bf16[2,4,8,512]{3,2,1,0:T(8,128)(2,1)} %bitcast.45) | data formatting | bytes 131072 | tf_op jit(solution)/shard_map/all_to_all | solution.py:53
  8.7 6.3 %all-to-all-start = ((bf16[16,4,512]{2,0,1:T(8,128)(2,1)}), bf16[16,4,512]{2,0,1:T(8,128)(2,1)S(1)}, u32[]{:S(2)}, u32[]{:S(2)}) async-start(bf16[16,4,512]{2,0,1:T(8,128)(2,1)} %bitcast.38), calls=%async_computation | async-start | bytes 131072 | tf_op jit(solution)/shard_map/all_to_all | solution.py:53
  15.1 9.0 %all-gather = bf16[8,8,4]{1,2,0:T(4,128)(2,1)S(1)} all-gather(bf16[1,8,4]{1,2,0:T(4,128)(2,1)} %bitcast.48), channel_id=1, replica_groups=mesh['patch'=8,'ulysses'=4] {'patch'}, dimensions={0}, use_global_device_ids=true | all-gather | bytes 576 | tf_op jit(solution)/shard_map/all_gather | solution.py:71
  24.1 0.1 copy.46
  24.2 8.7 %all-gather.1 = bf16[8,8,4]{1,2,0:T(4,128)(2,1)S(1)} all-gather(bf16[1,8,4]{1,2,0:T(4,128)(2,1)} %bitcast.49), channel_id=1, replica_groups=mesh['patch'=8,'ulysses'=4] {'patch'}, dimensions={0}, use_global_device_ids=true | all-gather | bytes 576 | tf_op jit(solution)/shard_map/all_gather | solution.py:72
  32.9 0.1 copy.47
  33.1 0.9 convert_bitcast_fusion.1
  34.0 0.9 convert_bitcast_fusion
  34.9 0.7 broadcast_bitcast_fusion
  35.6 9.9 %all_gather.16 = bf16[64,8,512]{2,1,0:T(8,128)(2,1)S(1)} all-gather(bf16[8,8,512]{2,1,0:T(8,128)(2,1)S(1)} %convert_bitcast_fusion.1), channel_id=1, replica_groups=mesh['patch'=8,'ulysses'=4] {'patch'}, dimensions={0}, use_global_device_ids=true | all-gather | bytes 589824 | tf_op jit(solution)/shard_map/all_gather | solution.py:69
  45.5 0.3 reshape.64
  45.9 0.6 copy.67
  46.5 5.0 %all-to-all-start.2 = ((bf16[16,4,512]{2,0,1:T(8,128)(2,1)}), bf16[16,4,512]{2,0,1:T(8,128)(2,1)S(1)}, u32[]{:S(2)}, u32[]{:S(2)}) async-start(bf16[16,4,512]{2,0,1:T(8,128)(2,1)} %bitcast.36), calls=%async_computation.2 | async-start | bytes 131072 | tf_op jit(solution)/shard_map/all_to_all | solution.py:54
  51.5 9.7 %all_gather.18 = bf16[64,8,512]{2,1,0:T(8,128)(2,1)S(1)} all-gather(bf16[8,8,512]{2,1,0:T(8,128)(2,1)S(1)} %convert_bitcast_fusion), channel_id=1, replica_groups=mesh['patch'=8,'ulysses'=4] {'patch'}, dimensions={0}, use_global_device_ids=true | all-gather | bytes 589824 | tf_op jit(solution)/shard_map/all_gather | solution.py:70
  61.2 0.3 reshape.66
  61.5 1.4 %reshape.63 = f32[512,4,128]{2,1,0:T(4,128)S(1)} reshape(bf16[512,512]{1,0:T(8,128)(2,1)} %param.13) | data formatting | bytes 1572864 | tf_op jit(solution)/shard_map/convert_element_type | solution.py:15
  62.9 2.4 %reshape.65 = f32[512,4,128]{2,1,0:T(4,128)} reshape(bf16[512,512]{1,0:T(8,128)(2,1)} %param.14) | data formatting | bytes 1572864 | tf_op jit(solution)/shard_map/convert_element_type | solution.py:15
  65.3 1.5 %copy.68 = bf16[2,4,8,512]{3,2,0,1:T(8,128)(2,1)} copy(bf16[2,4,8,512]{3,2,1,0:T(8,128)(2,1)} %bitcast.47) | data formatting | bytes 131072 | tf_op jit(solution)/shard_map/all_to_all | solution.py:52
  66.7 5.1 %all-to-all-start.1 = ((bf16[16,4,512]{2,0,1:T(8,128)(2,1)}), bf16[16,4,512]{2,0,1:T(8,128)(2,1)}, u32[]{:S(2)}, u32[]{:S(2)}) async-start(bf16[16,4,512]{2,0,1:T(8,128)(2,1)} %bitcast.42), calls=%async_computation.1 | async-start | bytes 131072 | tf_op jit(solution)/shard_map/all_to_all | solution.py:52
  71.8 0.1 broadcast_in_dim.23
  71.9 0.1 broadcast_in_dim.24
  72.0 0.9 tile.23
  72.9 4.8 %all-to-all-done.1 = bf16[16,4,512]{2,0,1:T(8,128)(2,1)} async-done(((bf16[16,4,512]{2,0,1:T(8,128)(2,1)}), bf16[16,4,512]{2,0,1:T(8,128)(2,1)}, u32[]{:S(2)}, u32[]{:S(2)}) %all-to-all-start.1) | async-done | bytes 65568 | tf_op jit(solution)/shard_map/all_to_all | solution.py:52
  77.7 1.5 %reshape.60 = bf16[64,4,128]{2,1,0:T(4,128)(2,1)} reshape(bf16[4,16,512]{2,1,0:T(8,128)(2,1)} %bitcast.5) | data formatting | bytes 131072 | tf_op jit(solution)/shard_map/reshape | solution.py:58
  79.2 4.3 %fusion.3 = (bf16[512,4,128]{2,1,0:T(4,128)(2,1)S(1)}, bf16[512,4,128]{2,1,0:T(4,128)(2,1)}) fusion(f32[512,4,128]{2,1,0:T(4,128)S(1)} %reshape.63, f32[512,4,128]{2,1,0:T(4,128)S(1)} %reshape.64, f32[512,4]{1,0:T(8,128)} %get-tuple-element.10, pred[512]{0:T(512)(128)(4,1)S(1)} %broadcast_in_dim.24, bf16[64,4,128]{2,1,0:T(4,128)(2,1)S(1)} %tile.20, ...), kind=kLoop, calls=%fused_computation.8 | loop fusion | flops 2097152 | bytes 5390848 | tf_op jit(solution)/shard_map/jit(_where)/select_n | solution.py:79
  83.5 0.4 fusion.16
  83.9 0.2 fusion.8
  84.1 0.0 all-gather.4.cloned.1.call-done
  84.2 3.7 %fusion = bf16[64,3072]{1,0:T(8,128)(2,1)} fusion(bf16[4,128,3072]{2,1,0:T(8,128)(2,1)} %bitcast.39, bf16[512,4,128]{2,1,0:T(4,128)(2,1)} %get-tuple-element.6, f32[4,64,512]{2,1,0:T(8,128)S(1)} %get-tuple-element.8, f32[4,64]{1,0:T(4,128)S(1)} %broadcast_maximum_fusion, f32[4,64]{1,0:T(4,128)S(1)} %fusion.8), kind=kOutput, calls=%fused_computation.1 | convolution fusion | flops 235405312 | bytes 4589568 | tf_op jit(solution)/shard_map/hqd,hdc->qc/dot_general | solution.py:90
  87.8 0.0 reduce-scatter.2.cloned.1.call-update
  87.9 18.3 %reduce-scatter.2.cloned.1.call-done = bf16[16,3072]{1,0:T(8,128)(2,1)} async-done(((bf16[64,3072]{1,0:T(8,128)(2,1)}), bf16[16,3072]{1,0:T(8,128)(2,1)}) %reduce-scatter.2.cloned.1.call-update) | async-done | bytes 98320 | tf_op jit(solution)/shard_map/reduce_scatter | solution.py:89
  (15 shorter events, 0.1 us)
Async XLA Ops:
  6.5 39.3 %copy-start.2 = (bf16[16,2048]{1,0:T(8,128)(2,1)S(1)}, bf16[16,2048]{1,0:T(8,128)(2,1)}, u32[]{:S(2)}) copy-start(bf16[16,2048]{1,0:T(8,128)(2,1)} %param.12) | copy-start | bytes 196612
  6.5 77.6 %all-gather.4.cloned.1.call-start = ((), (), s32[]{:S(2)}) async-start(), calls=%async_computation.4 | async-start | bytes 3538944 | tf_op jit(solution)/shard_map/all_gather | solution.py:87
  8.7 37.8 %all-to-all-start = ((bf16[16,4,512]{2,0,1:T(8,128)(2,1)}), bf16[16,4,512]{2,0,1:T(8,128)(2,1)S(1)}, u32[]{:S(2)}, u32[]{:S(2)}) async-start(bf16[16,4,512]{2,0,1:T(8,128)(2,1)} %bitcast.38), calls=%async_computation | async-start | bytes 131072 | tf_op jit(solution)/shard_map/all_to_all | solution.py:53
  46.5 20.2 %all-to-all-start.2 = ((bf16[16,4,512]{2,0,1:T(8,128)(2,1)}), bf16[16,4,512]{2,0,1:T(8,128)(2,1)S(1)}, u32[]{:S(2)}, u32[]{:S(2)}) async-start(bf16[16,4,512]{2,0,1:T(8,128)(2,1)} %bitcast.36), calls=%async_computation.2 | async-start | bytes 131072 | tf_op jit(solution)/shard_map/all_to_all | solution.py:54
  66.7 5.3 %copy-start.1 = (bf16[16,4,512]{2,0,1:T(8,128)(2,1)}, bf16[16,4,512]{2,0,1:T(8,128)(2,1)S(1)}, u32[]{:S(2)}) copy-start(bf16[16,4,512]{2,0,1:T(8,128)(2,1)S(1)} %all-to-all-done.2) | copy-start | bytes 196612
  66.7 10.9 %all-to-all-start.1 = ((bf16[16,4,512]{2,0,1:T(8,128)(2,1)}), bf16[16,4,512]{2,0,1:T(8,128)(2,1)}, u32[]{:S(2)}, u32[]{:S(2)}) async-start(bf16[16,4,512]{2,0,1:T(8,128)(2,1)} %bitcast.42), calls=%async_computation.1 | async-start | bytes 131072 | tf_op jit(solution)/shard_map/all_to_all | solution.py:52
  71.8 34.3 %reduce-scatter.2.cloned.1.call-start = ((), (), s32[]{:S(2)}) async-start(), calls=%async_computation.5 | async-start | bytes 491520 | tf_op jit(solution)/shard_map/reduce_scatter | solution.py:89
  79.2 4.3 %copy-start = (bf16[64,4,128]{2,1,0:T(4,128)(2,1)S(1)}, bf16[64,4,128]{2,1,0:T(4,128)(2,1)}, u32[]{:S(2)}) copy-start(bf16[64,4,128]{2,1,0:T(4,128)(2,1)} %reshape.60) | copy-start | bytes 196612
Sparse Core Ops, SparseCore 0:
  9.2 36.7 all-gather.3
  88.0 18.1 reduce-scatter.1
where the time goes:
time: 114 us; the launch traced here: 113 us
  blocking collectives  37.3 us (33%)
  waiting for transfers between devices  23.9 us (21%)
  starting transfers between devices  16.4 us (14%)
  between operations  13.5 us (12%)
  local copies, waits for them, and re-layouts  11.5 us (10%)
  other arithmetic  6.42 us (6%)
  matrix products  4.05 us (4%)
    reduce_scatter x1, waiting for transfers between devices, on_device(): lax.psum_scatter(jnp.einsum('hqd,hdc->qc', attended, weight_heads, prefer...  18.3 us
    all_gather x1, blocking collectives, on_device(): segment_keys = lax.all_gather(key_block, 'patch', axis=0, tiled=True)  9.88 us
    all_gather x1, blocking collectives, on_device(): piece_values = lax.all_gather(value_block, 'patch', axis=0, tiled=True)  9.69 us
    all_gather x1, blocking collectives, on_device(): lax.all_gather(key_code_scales, 'patch', axis=0, tiled=True)  9.02 us
    all_gather x1, blocking collectives, on_device(): piece_vscale = lax.all_gather(value_scales, 'patch', axis=0, tiled=True)  8.73 us
    all_to_all x1, starting transfers between devices, on_device(): lax.all_to_all(fresh_keys, 'ulysses', split_axis=1, concat_axis=0, tiled=...  6.32 us
    all_to_all x1, starting transfers between devices, on_device(): lax.all_to_all(fresh_queries, 'ulysses', split_axis=1, concat_axis=0, til...  5.09 us
    all_to_all x1, starting transfers between devices, on_device(): lax.all_to_all(fresh_values, 'ulysses', split_axis=1, concat_axis=0, tile...  5.02 us
  transfers between devices with their start and end apart: 5, of which 2 were waited for; matrix products, arithmetic and copies ran while one was open for 16% of the time, Pallas kernels for 0%

commit v1 on v0

v1 whole, which is shorter than its diff:
```python
import functools
import math

import jax
import jax.numpy as jnp
from jax import lax
from jax.experimental import pallas as pl
from jax.experimental.pallas import tpu as pltpu
from jax.sharding import PartitionSpec as P

HEAD_DIM = 128
BLOCK = 8
MESH = pl.DeviceIdType.MESH


def send(src, dst, send_sem, recv_sem, target, here):
    same = jnp.logical_and(target[0] == here[0], target[1] == here[1])

    @pl.when(same)
    def _():
        pltpu.make_async_copy(src, dst, recv_sem).start()

    @pl.when(jnp.logical_not(same))
    def _():
        pltpu.make_async_remote_copy(
            src, dst, send_sem, recv_sem, device_id=target, device_id_type=MESH
        ).start()


def finish_send(src, dst, send_sem, recv_sem, target, here):
    same = jnp.logical_and(target[0] == here[0], target[1] == here[1])

    @pl.when(jnp.logical_not(same))
    def _():
        pltpu.make_async_remote_copy(
            src, dst, send_sem, recv_sem, device_id=target, device_id_type=MESH
        ).wait_send()


def wait_bytes(buffer, sem):
    pltpu.make_async_copy(buffer, buffer, sem).wait()


def kernel(
    patches, groups,
    key_scales, value_scales,
    fresh_q, fresh_k, fresh_v, old_k, old_v, codes_k, codes_v, weight,
    out,
    fresh_in, old_in, codes_in, weight_in,
    fresh_out, fresh_got, seen_out, seen_got, key_work, value_work,
    attended_out, attended_got, terms_out, terms_got,
    load_sem, fresh_send, fresh_recv, seen_send, seen_recv,
    attended_send, attended_recv, terms_send, terms_recv,
):
    p = lax.axis_index("patch")
    u = lax.axis_index("ulysses")
    here = (p, u)
    rows = fresh_q.shape[0]
    span = rows * groups
    heads = fresh_q.shape[1] // HEAD_DIM
    local = heads // groups
    ranks = patches // local
    my_head = p // ranks
    my_rank = lax.rem(p, ranks)

    loads = [
        pltpu.make_async_copy(source, fresh_in.at[i], load_sem.at[i])
        for i, source in enumerate((fresh_q, fresh_k, fresh_v))
    ]
    first = pl.multiple_of(p * span, span)
    loads.append(pltpu.make_async_copy(old_k.at[pl.ds(first, span)], old_in.at[0], load_sem.at[3]))
    loads.append(pltpu.make_async_copy(old_v.at[pl.ds(first, span)], old_in.at[1], load_sem.at[4]))
    loads.append(pltpu.make_async_copy(codes_k, codes_in.at[0], load_sem.at[5]))
    loads.append(pltpu.make_async_copy(codes_v, codes_in.at[1], load_sem.at[6]))
    loads.append(pltpu.make_async_copy(weight, weight_in, load_sem.at[7]))
    for load in loads:
        load.start()

    barrier = pltpu.get_barrier_semaphore()
    devices = patches * groups

    def greet(i, carry):
        to_p, to_u = i // groups, lax.rem(i, groups)

        @pl.when(jnp.logical_not(jnp.logical_and(to_p == p, to_u == u)))
        def _():
            pl.semaphore_signal(barrier, inc=1, device_id=(to_p, to_u), device_id_type=MESH)

        return carry

    lax.fori_loop(0, devices, greet, 0)

    for load in loads[:3]:
        load.wait()
    for h in range(heads):
        for i in range(3):
            fresh_out[h, i] = fresh_in[i, :, h * HEAD_DIM:(h + 1) * HEAD_DIM]
    for load in loads[3:7]:
        load.wait()
    block_of = lax.broadcasted_iota(jnp.int32, (span, span // BLOCK), 0) // BLOCK
    pick = (block_of == lax.broadcasted_iota(jnp.int32, (span, span // BLOCK), 1)).astype(jnp.float32)
    for i, scales in enumerate((key_scales, value_scales)):
        wide = jnp.dot(
            pick, scales[...].astype(jnp.float32), preferred_element_type=jnp.float32
        )
        for l in range(local):
            cols = slice(l * HEAD_DIM, (l + 1) * HEAD_DIM)
            seen_out[l, i] = (
                old_in[i, :, cols].astype(jnp.float32)
                + wide[:, l:l + 1] * codes_in[i, :, cols].astype(jnp.float32)
            ).astype(jnp.bfloat16)

    pl.semaphore_wait(barrier, devices - 1)

    def fresh_args(i):
        h = lax.rem(u * local + local + i, heads)
        target = (lax.rem(h, local) * ranks + p // local, h // local)
        return (fresh_out.at[h], fresh_got.at[lax.rem(p, local), u],
                fresh_send.at[h], fresh_recv, target, here)

    def seen_args(i):
        to = lax.rem(p + 1 + i, patches)
        return (seen_out.at[to // ranks], seen_got.at[p], seen_send.at[to], seen_recv, (to, u), here)

    def start_fresh(i, carry):
        send(*fresh_args(i))
        return carry

    def start_seen(i, carry):
        send(*seen_args(i))
        return carry

    lax.fori_loop(0, heads, start_fresh, 0)
    lax.fori_loop(0, patches, start_seen, 0)
    wait_bytes(seen_got, seen_recv)
    for i in range(local):
        key_work[i] = seen_got[:, 0].reshape(patches * span, HEAD_DIM)
        value_work[i] = seen_got[:, 1].reshape(patches * span, HEAD_DIM)
    wait_bytes(fresh_got, fresh_recv)

    scale_qk = 1.0 / math.sqrt(HEAD_DIM)

    def attended_args(slot, patch, i):
        to = lax.rem(p + 1 + i, patches)
        return (attended_out.at[slot], attended_got.at[patch, my_head],
                attended_send.at[slot, to], attended_recv.at[patch], (to, u), here)

    def attend(slot):
        index = lax.rem(slot + u, local)
        patch = my_rank * local + index
        query = fresh_got[index, :, 0].reshape(span, HEAD_DIM)
        own = pl.ds(pl.multiple_of(patch * span, span), span)
        key_work[slot, own] = fresh_got[index, :, 1].reshape(span, HEAD_DIM)
        value_work[slot, own] = fresh_got[index, :, 2].reshape(span, HEAD_DIM)
        scores = lax.dot_general(
            query, key_work[slot], (((1,), (1,)), ((), ())), preferred_element_type=jnp.float32
        ) * scale_qk
        top = jnp.max(scores, axis=1, keepdims=True)
        weights = jnp.exp(scores - top)
        total = jnp.sum(weights, axis=1, keepdims=True)
        mixed = jnp.dot(
            weights.astype(jnp.bfloat16), value_work[slot], preferred_element_type=jnp.float32
        )
        attended_out[slot] = (mixed / total).astype(jnp.bfloat16)

        def start(i, carry):
            send(*attended_args(slot, patch, i))
            return carry

        lax.fori_loop(0, patches, start, 0)

    def terms_args(patch, i):
        to = lax.rem(u + 1 + i, groups)
        return (terms_out.at[patch, to], terms_got.at[u, p],
                terms_send.at[patch, to], terms_recv, (patch, to), here)

    def project(slot):
        index = lax.rem(slot + u, local)
        for r in range(ranks):
            patch = r * local + index
            wait_bytes(attended_got.at[patch], attended_recv.at[patch])
            gathered = jnp.concatenate([attended_got[patch, l] for l in range(local)], axis=1)
            terms = jnp.dot(gathered, weight_in[...], preferred_element_type=jnp.float32)
            terms_out[patch] = terms.astype(jnp.bfloat16).reshape(groups, rows, terms.shape[1])

            def start(i, carry):
                send(*terms_args(patch, i))
                return carry

            lax.fori_loop(0, groups, start, 0)

    for slot in range(local):
        attend(slot)
    loads[7].wait()
    for slot in range(local):
        project(slot)

    def end_fresh(i, carry):
        finish_send(*fresh_args(i))
        return carry

    def end_seen(i, carry):
        finish_send(*seen_args(i))
        return carry

    lax.fori_loop(0, heads, end_fresh, 0)
    lax.fori_loop(0, patches, end_seen, 0)
    for slot in range(local):
        patch = my_rank * local + lax.rem(slot + u, local)

        def end(i, carry):
            finish_send(*attended_args(slot, patch, i))
            return carry

        lax.fori_loop(0, patches, end, 0)

    def end_terms(i, carry):
        finish_send(*terms_args(i // groups, lax.rem(i, groups)))
        return carry

    wait_bytes(terms_got, terms_recv)
    columns = weight.shape[1]
    for q in range(patches):
        total = terms_got[0, q].astype(jnp.float32)
        for g in range(1, groups):
            total = total + terms_got[g, q].astype(jnp.float32)
        out[:, q * columns:(q + 1) * columns] = total.astype(jnp.bfloat16)
    lax.fori_loop(0, patches * groups, end_terms, 0)


def solution(mesh):
    patches, groups = mesh.shape["patch"], mesh.shape["ulysses"]

    def on_device(
        fresh_queries, fresh_keys, fresh_values, outdated_keys, stale_values,
        key_codes, value_codes, key_code_scales, value_scales, out_weight,
    ):
        rows, width = fresh_queries.shape
        span = rows * groups
        heads = width // HEAD_DIM
        local = heads // groups
        depth, columns = out_weight.shape
        bf16, f32 = jnp.bfloat16, jnp.float32
        vmem = pl.BlockSpec(memory_space=pltpu.VMEM)
        hbm = pl.BlockSpec(memory_space=pl.ANY)
        dma = pltpu.SemaphoreType.DMA
        return pl.pallas_call(
            functools.partial(kernel, patches, groups),
            out_shape=jax.ShapeDtypeStruct((rows, patches * columns), bf16),
            in_specs=[vmem] * 2 + [hbm] * 8,
            out_specs=vmem,
            scratch_shapes=[
                pltpu.VMEM((3, rows, width), bf16),
                pltpu.VMEM((2, span, depth), bf16),
                pltpu.VMEM((2, span, depth), jnp.int32),
                pltpu.VMEM((depth, columns), bf16),
                pltpu.VMEM((heads, 3, rows, HEAD_DIM), bf16),
                pltpu.VMEM((local, groups, 3, rows, HEAD_DIM), bf16),
                pltpu.VMEM((local, 2, span, HEAD_DIM), bf16),
                pltpu.VMEM((patches, 2, span, HEAD_DIM), bf16),
                pltpu.VMEM((local, patches * span, HEAD_DIM), bf16),
                pltpu.VMEM((local, patches * span, HEAD_DIM), bf16),
                pltpu.VMEM((local, span, HEAD_DIM), bf16),
                pltpu.VMEM((patches, local, span, HEAD_DIM), bf16),
                pltpu.VMEM((patches, groups, rows, columns), bf16),
                pltpu.VMEM((groups, patches, rows, columns), bf16),
                dma((8,)), dma((heads,)), dma, dma((patches,)), dma,
                dma((local, patches)), dma((patches,)), dma((patches, groups)), dma,
            ],
            compiler_params=pltpu.CompilerParams(
                collective_id=0, has_side_effects=True, vmem_limit_bytes=48 * 1024 * 1024
            ),
        )(
            key_code_scales, value_scales, fresh_queries, fresh_keys, fresh_values,
            outdated_keys, stale_values, key_codes, value_codes, out_weight,
        )

    return jax.shard_map(
        on_device,
        mesh=mesh,
        in_specs=(
            P(("patch", "ulysses"), None),
            P(("patch", "ulysses"), None),
            P(("patch", "ulysses"), None),
            P(None, "ulysses"),
            P(None, "ulysses"),
            P("patch", "ulysses"),
            P("patch", "ulysses"),
            P("patch", "ulysses"),
            P("patch", "ulysses"),
            P("ulysses", "patch"),
        ),
        out_specs=P(("patch", "ulysses"), None),
        check_vma=False,
    )
```

time: 114 us -> 40 us (0.35)
  the two profiles are of different devices: /device:TPU:0 before, /device:TPU:1 now
where the time goes in v1:
time: 40 us; the launch traced here: 39.6 us
  Pallas kernels  30.6 us (76%)
  local copies, waits for them, and re-layouts  8.92 us (22%)
    pallas_call x1, Pallas kernels, on_device(): pl.pallas_call(functools.partial(kernel, patches, groups), out_shape=jax....  30.6 us
    unnamed x21, local copies, waits for them, and re-layouts  8.92 us

profile of v1, /device:TPU:1, one launch (start us, length us, event | category | flops | bytes accessed | tf_op | source)
XLA Modules:
  0.0 39.6 jit_solution(13872202146832471221)
XLA Ops:
  0.0 0.0 copy-start.8
  0.0 0.8 %copy.11.key_scales = bf16[8,4]{1,0:T(8,128)(2,1)S(1)} copy(bf16[8,4]{0,1:T(4,128)(2,1)} %param.17) | data formatting | bytes 128 | tf_op args[7]
  0.8 0.0 copy-done.8
  0.8 0.1 copy.12.value_scales
  0.9 0.0 copy-start
  0.9 1.0 %copy-done = bf16[512,512]{1,0:T(8,128)(2,1)S(1)} copy-done((bf16[512,512]{1,0:T(8,128)(2,1)S(1)}, bf16[512,512]{1,0:T(8,128)(2,1)}, u32[]{:S(2)}) %copy-start) | copy-done | bytes 524312
  1.9 0.0 copy-start.1
  1.9 1.0 %copy-done.1 = bf16[512,512]{1,0:T(8,128)(2,1)S(1)} copy-done((bf16[512,512]{1,0:T(8,128)(2,1)S(1)}, bf16[512,512]{1,0:T(8,128)(2,1)}, u32[]{:S(2)}) %copy-start.1) | copy-done | bytes 524312
  3.0 0.0 copy-start.2
  3.0 1.0 %copy-done.2 = bf16[512,384]{1,0:T(8,128)(2,1)S(1)} copy-done((bf16[512,384]{1,0:T(8,128)(2,1)S(1)}, bf16[512,384]{1,0:T(8,128)(2,1)}, u32[]{:S(2)}) %copy-start.2) | copy-done | bytes 393240
  4.0 0.0 copy-start.3
  4.0 0.9 %copy-done.3 = s32[64,512]{1,0:T(8,128)S(1)} copy-done((s32[64,512]{1,0:T(8,128)S(1)}, s32[64,512]{1,0:T(8,128)}, u32[]{:S(2)}) %copy-start.3) | copy-done | bytes 131096
  4.9 0.0 copy-start.4
  4.9 0.9 %copy-done.4 = s32[64,512]{1,0:T(8,128)S(1)} copy-done((s32[64,512]{1,0:T(8,128)S(1)}, s32[64,512]{1,0:T(8,128)}, u32[]{:S(2)}) %copy-start.4) | copy-done | bytes 131096
  5.8 0.0 copy-start.5
  5.8 0.8 %copy-done.5 = bf16[16,2048]{1,0:T(8,128)(2,1)S(1)} copy-done((bf16[16,2048]{1,0:T(8,128)(2,1)S(1)}, bf16[16,2048]{1,0:T(8,128)(2,1)}, u32[]{:S(2)}) %copy-start.5) | copy-done | bytes 65560
  6.6 0.0 copy-start.6
  6.6 0.8 %copy-done.6 = bf16[16,2048]{1,0:T(8,128)(2,1)S(1)} copy-done((bf16[16,2048]{1,0:T(8,128)(2,1)S(1)}, bf16[16,2048]{1,0:T(8,128)(2,1)}, u32[]{:S(2)}) %copy-start.6) | copy-done | bytes 65560
  7.5 0.0 copy-start.7
  7.5 0.8 %copy-done.7 = bf16[16,2048]{1,0:T(8,128)(2,1)S(1)} copy-done((bf16[16,2048]{1,0:T(8,128)(2,1)S(1)}, bf16[16,2048]{1,0:T(8,128)(2,1)}, u32[]{:S(2)}) %copy-start.7) | copy-done | bytes 65560
  8.3 30.6 %shard_map.100 = bf16[16,3072]{1,0:T(8,128)(2,1)S(1)} custom-call(bf16[8,4]{1,0:T(8,128)(2,1)S(1)} %copy.11.key_scales, bf16[8,4]{1,0:T(8,128)(2,1)S(1)} %copy.12.value_scales, bf16[16,2048]{1,0:T(8,128)(2,1)S(1)} %copy-done.5, bf16[16,2048]{1,0:T(8,128)(2,1)S(1)} %copy-done.6, bf16[16,2048]{1,0:T(8,128)(2,1)S(1)} %copy-done.7, ...), custom_call_target="tpu_custom_call" | custom-call | tf_op jit(solution)/shard_map/pallas_call | solution.py:247
  38.9 0.6 %copy.14 = bf16[16,3072]{1,0:T(8,128)(2,1)} copy(bf16[16,3072]{1,0:T(8,128)(2,1)S(1)} %shard_map.100) | data formatting | bytes 196608
Async XLA Ops:
  0.0 0.8 %copy-start.8 = (bf16[8,4]{0,1:T(4,128)(2,1)S(1)}, bf16[8,4]{0,1:T(4,128)(2,1)}, u32[]{:S(2)}) copy-start(bf16[8,4]{0,1:T(4,128)(2,1)} %param.18) | copy-start | bytes 196
  0.9 1.0 %copy-start = (bf16[512,512]{1,0:T(8,128)(2,1)S(1)}, bf16[512,512]{1,0:T(8,128)(2,1)}, u32[]{:S(2)}) copy-start(bf16[512,512]{1,0:T(8,128)(2,1)} %old_k.1) | copy-start | bytes 1572868
  1.9 1.0 %copy-start.1 = (bf16[512,512]{1,0:T(8,128)(2,1)S(1)}, bf16[512,512]{1,0:T(8,128)(2,1)}, u32[]{:S(2)}) copy-start(bf16[512,512]{1,0:T(8,128)(2,1)} %old_v.1) | copy-start | bytes 1572868
  3.0 1.0 %copy-start.2 = (bf16[512,384]{1,0:T(8,128)(2,1)S(1)}, bf16[512,384]{1,0:T(8,128)(2,1)}, u32[]{:S(2)}) copy-start(bf16[512,384]{1,0:T(8,128)(2,1)} %weight.1) | copy-start | bytes 1179652
  4.0 0.9 %copy-start.3 = (s32[64,512]{1,0:T(8,128)S(1)}, s32[64,512]{1,0:T(8,128)}, u32[]{:S(2)}) copy-start(s32[64,512]{1,0:T(8,128)} %codes_k.1) | copy-start | bytes 393220
  4.9 0.9 %copy-start.4 = (s32[64,512]{1,0:T(8,128)S(1)}, s32[64,512]{1,0:T(8,128)}, u32[]{:S(2)}) copy-start(s32[64,512]{1,0:T(8,128)} %codes_v.1) | copy-start | bytes 393220
  5.8 0.8 %copy-start.5 = (bf16[16,2048]{1,0:T(8,128)(2,1)S(1)}, bf16[16,2048]{1,0:T(8,128)(2,1)}, u32[]{:S(2)}) copy-start(bf16[16,2048]{1,0:T(8,128)(2,1)} %fresh_q.1) | copy-start | bytes 196612
  6.6 0.8 %copy-start.6 = (bf16[16,2048]{1,0:T(8,128)(2,1)S(1)}, bf16[16,2048]{1,0:T(8,128)(2,1)}, u32[]{:S(2)}) copy-start(bf16[16,2048]{1,0:T(8,128)(2,1)} %fresh_k.1) | copy-start | bytes 196612
  7.5 0.8 %copy-start.7 = (bf16[16,2048]{1,0:T(8,128)(2,1)S(1)}, bf16[16,2048]{1,0:T(8,128)(2,1)}, u32[]{:S(2)}) copy-start(bf16[16,2048]{1,0:T(8,128)(2,1)} %fresh_v.1) | copy-start | bytes 196612

commit v2 on v1

--- a/solution.py
+++ b/solution.py
@@ -100,8 +100,9 @@
     block_of = lax.broadcasted_iota(jnp.int32, (span, span // BLOCK), 0) // BLOCK
     pick = (block_of == lax.broadcasted_iota(jnp.int32, (span, span // BLOCK), 1)).astype(jnp.float32)
     for i, scales in enumerate((key_scales, value_scales)):
-        wide = jnp.dot(
-            pick, scales[...].astype(jnp.float32), preferred_element_type=jnp.float32
+        wide = lax.dot_general(
+            pick, scales[...].astype(jnp.float32), (((1,), (1,)), ((), ())),
+            preferred_element_type=jnp.float32,
         )
         for l in range(local):
             cols = slice(l * HEAD_DIM, (l + 1) * HEAD_DIM)
@@ -242,7 +243,7 @@
         depth, columns = out_weight.shape
         bf16, f32 = jnp.bfloat16, jnp.float32
         vmem = pl.BlockSpec(memory_space=pltpu.VMEM)
-        hbm = pl.BlockSpec(memory_space=pl.ANY)
+        hbm = pl.BlockSpec(memory_space=pltpu.HBM)
         dma = pltpu.SemaphoreType.DMA
         return pl.pallas_call(
             functools.partial(kernel, patches, groups),
@@ -268,10 +269,10 @@
                 dma((local, patches)), dma((patches,)), dma((patches, groups)), dma,
             ],
             compiler_params=pltpu.CompilerParams(
-                collective_id=0, has_side_effects=True, vmem_limit_bytes=48 * 1024 * 1024
+                collective_id=0, has_side_effects=True, vmem_limit_bytes=60 * 1024 * 1024
             ),
         )(
-            key_code_scales, value_scales, fresh_queries, fresh_keys, fresh_values,
+            key_code_scales.T, value_scales.T, fresh_queries, fresh_keys, fresh_values,
             outdated_keys, stale_values, key_codes, value_codes, out_weight,
         )
 

time: 40 us -> 32.7 us (0.82)
  local copies, waits for them, and re-layouts: 8.92 us -> 1.54 us
    unnamed x21 -> x1, local copies, waits for them, and re-layouts: 8.92 us -> 1.54 us
where the time goes in v2:
time: 32.7 us; the launch traced here: 32.5 us
  Pallas kernels  31 us (95%)
  local copies, waits for them, and re-layouts  1.54 us (5%)
    pallas_call x1, Pallas kernels, on_device(): pl.pallas_call(functools.partial(kernel, patches, groups), out_shape=jax....  31 us
    unnamed x1, local copies, waits for them, and re-layouts  1.54 us

profile of v2, /device:TPU:1, one launch (start us, length us, event | category | flops | bytes accessed | tf_op | source)
XLA Modules:
  0.0 32.5 jit_solution(12541363966678563035)
XLA Ops:
  0.0 31.0 %shard_map.100 = bf16[16,3072]{1,0:T(8,128)(2,1)} custom-call(bf16[4,8]{1,0:T(4,128)(2,1)} %bitcast.2, bf16[4,8]{1,0:T(4,128)(2,1)} %bitcast.3, bf16[16,2048]{1,0:T(8,128)(2,1)} %fresh_q.1, bf16[16,2048]{1,0:T(8,128)(2,1)} %fresh_k.1, bf16[16,2048]{1,0:T(8,128)(2,1)} %fresh_v.1, bf16[512,512]{1,0:T(8,128)(2,1)} %old_k.1, bf16[512,512]{1,0:T(8,128)(2,1)} %old_v.1, ...), custom_call_target="tpu_custom_call" | custom-call | tf_op jit(solution)/shard_map/pallas_call | solution.py:248
  31.0 1.5 %copy.12 = bf16[16,3072]{1,0:T(8,128)(2,1)} copy(bf16[16,3072]{1,0:T(8,128)(2,1)} %shard_map.100) | data formatting | bytes 196608

commit v3 on v2

--- a/solution.py
+++ b/solution.py
@@ -46,10 +46,11 @@
     key_scales, value_scales,
     fresh_q, fresh_k, fresh_v, old_k, old_v, codes_k, codes_v, weight,
     out,
-    fresh_in, old_in, codes_in, weight_in,
+    fresh_in, old_in, codes_in, weight_got,
     fresh_out, fresh_got, seen_out, seen_got, key_work, value_work,
     attended_out, attended_got, terms_out, terms_got,
-    load_sem, fresh_send, fresh_recv, seen_send, seen_recv,
+    load_sem, weight_send, weight_recv, fresh_send, fresh_recv,
+    seen_send, seen_recv, pass_send, pass_recv,
     attended_send, attended_recv, terms_send, terms_recv,
 ):
     p = lax.axis_index("patch")
@@ -72,7 +73,7 @@
     loads.append(pltpu.make_async_copy(old_v.at[pl.ds(first, span)], old_in.at[1], load_sem.at[4]))
     loads.append(pltpu.make_async_copy(codes_k, codes_in.at[0], load_sem.at[5]))
     loads.append(pltpu.make_async_copy(codes_v, codes_in.at[1], load_sem.at[6]))
-    loads.append(pltpu.make_async_copy(weight, weight_in, load_sem.at[7]))
+    loads.append(pltpu.make_async_copy(weight, weight_got.at[my_rank], load_sem.at[7]))
     for load in loads:
         load.start()
 
@@ -120,37 +121,67 @@
                 fresh_send.at[h], fresh_recv, target, here)
 
     def seen_args(i):
-        to = lax.rem(p + 1 + i, patches)
-        return (seen_out.at[to // ranks], seen_got.at[p], seen_send.at[to], seen_recv, (to, u), here)
+        m = lax.rem(my_head + i, local)
+        return (seen_out.at[m], seen_got.at[my_rank, my_head], seen_send.at[m],
+                seen_recv.at[my_head], (m * ranks + my_rank, u), here)
+
+    def pass_args(m, i):
+        to = lax.rem(my_rank + 1 + i, ranks)
+        block = seen_got.at[my_rank, m]
+        return (block, block, pass_send.at[m, to], pass_recv.at[my_rank],
+                (my_head * ranks + to, u), here)
+
+    def weight_args(i):
+        to = lax.rem(my_rank + 1 + i, ranks)
+        return (weight, weight_got.at[my_rank], weight_send.at[to], weight_recv.at[my_rank],
+                (my_head * ranks + to, u), here)
 
     def start_fresh(i, carry):
         send(*fresh_args(i))
         return carry
 
-    def start_seen(i, carry):
+    def start_weight(i, carry):
+        send(*weight_args(i))
+        return carry
+
+    for i in range(local):
         send(*seen_args(i))
-        return carry
-
     lax.fori_loop(0, heads, start_fresh, 0)
-    lax.fori_loop(0, patches, start_seen, 0)
-    wait_bytes(seen_got, seen_recv)
     for i in range(local):
-        key_work[i] = seen_got[:, 0].reshape(patches * span, HEAD_DIM)
-        value_work[i] = seen_got[:, 1].reshape(patches * span, HEAD_DIM)
+        m = lax.rem(my_head + local - i, local)
+        wait_bytes(seen_got.at[my_rank, m], seen_recv.at[m])
+
+        def start_pass(i, carry):
+            send(*pass_args(m, i))
+            return carry
+
+        lax.fori_loop(0, ranks - 1, start_pass, 0)
+    lax.fori_loop(0, ranks - 1, start_weight, 0)
+
+    def wait_pass(i, carry):
+        source = lax.rem(my_rank + 1 + i, ranks)
+        wait_bytes(seen_got.at[source], pass_recv.at[source])
+        return carry
+
+    lax.fori_loop(0, ranks - 1, wait_pass, 0)
+    for i in range(local):
+        key_work[i] = seen_got[:, :, 0].reshape(patches * span, HEAD_DIM)
+        value_work[i] = seen_got[:, :, 1].reshape(patches * span, HEAD_DIM)
     wait_bytes(fresh_got, fresh_recv)
 
     scale_qk = 1.0 / math.sqrt(HEAD_DIM)
 
-    def attended_args(slot, patch, i):
-        to = lax.rem(p + 1 + i, patches)
-        return (attended_out.at[slot], attended_got.at[patch, my_head],
-                attended_send.at[slot, to], attended_recv.at[patch], (to, u), here)
+    def attended_args(slot, index, i):
+        m = lax.rem(my_head + 1 + i, local)
+        return (attended_out.at[slot], attended_got.at[index, my_head],
+                attended_send.at[slot, m], attended_recv.at[index], (m * ranks + my_rank, u), here)
 
     def attend(slot):
         index = lax.rem(slot + u, local)
         patch = my_rank * local + index
         query = fresh_got[index, :, 0].reshape(span, HEAD_DIM)
-        own = pl.ds(pl.multiple_of(patch * span, span), span)
+        place = lax.rem(patch, ranks) * local + patch // ranks
+        own = pl.ds(pl.multiple_of(place * span, span), span)
         key_work[slot, own] = fresh_got[index, :, 1].reshape(span, HEAD_DIM)
         value_work[slot, own] = fresh_got[index, :, 2].reshape(span, HEAD_DIM)
         scores = lax.dot_general(
@@ -165,68 +196,79 @@
         attended_out[slot] = (mixed / total).astype(jnp.bfloat16)
 
         def start(i, carry):
-            send(*attended_args(slot, patch, i))
-            return carry
-
-        lax.fori_loop(0, patches, start, 0)
-
-    def terms_args(patch, i):
+            send(*attended_args(slot, index, i))
+            return carry
+
+        lax.fori_loop(0, local, start, 0)
+
+    def terms_args(index, i):
         to = lax.rem(u + 1 + i, groups)
-        return (terms_out.at[patch, to], terms_got.at[u, p],
-                terms_send.at[patch, to], terms_recv, (patch, to), here)
+        return (terms_out.at[index, to], terms_got.at[u, my_head], terms_send.at[index, to],
+                terms_recv, (my_rank * local + index, to), here)
 
     def project(slot):
         index = lax.rem(slot + u, local)
+        wait_bytes(attended_got.at[index], attended_recv.at[index])
+        gathered = jnp.concatenate([attended_got[index, l] for l in range(local)], axis=1)
         for r in range(ranks):
-            patch = r * local + index
-            wait_bytes(attended_got.at[patch], attended_recv.at[patch])
-            gathered = jnp.concatenate([attended_got[patch, l] for l in range(local)], axis=1)
-            terms = jnp.dot(gathered, weight_in[...], preferred_element_type=jnp.float32)
-            terms_out[patch] = terms.astype(jnp.bfloat16).reshape(groups, rows, terms.shape[1])
-
-            def start(i, carry):
-                send(*terms_args(patch, i))
-                return carry
-
-            lax.fori_loop(0, groups, start, 0)
+            terms = jnp.dot(gathered, weight_got[r], preferred_element_type=jnp.float32)
+            terms_out[index, :, r] = terms.astype(jnp.bfloat16).reshape(groups, rows, terms.shape[1])
+
+        def start(i, carry):
+            send(*terms_args(index, i))
+            return carry
+
+        lax.fori_loop(0, groups, start, 0)
 
     for slot in range(local):
         attend(slot)
     loads[7].wait()
+
+    def wait_weight(i, carry):
+        source = lax.rem(my_rank + 1 + i, ranks)
+        wait_bytes(weight_got.at[source], weight_recv.at[source])
+        return carry
+
+    lax.fori_loop(0, ranks - 1, wait_weight, 0)
     for slot in range(local):
         project(slot)
-
-    def end_fresh(i, carry):
-        finish_send(*fresh_args(i))
-        return carry
-
-    def end_seen(i, carry):
-        finish_send(*seen_args(i))
-        return carry
-
-    lax.fori_loop(0, heads, end_fresh, 0)
-    lax.fori_loop(0, patches, end_seen, 0)
-    for slot in range(local):
-        patch = my_rank * local + lax.rem(slot + u, local)
-
-        def end(i, carry):
-            finish_send(*attended_args(slot, patch, i))
-            return carry
-
-        lax.fori_loop(0, patches, end, 0)
-
-    def end_terms(i, carry):
-        finish_send(*terms_args(i // groups, lax.rem(i, groups)))
-        return carry
 
     wait_bytes(terms_got, terms_recv)
     columns = weight.shape[1]
     for q in range(patches):
-        total = terms_got[0, q].astype(jnp.float32)
+        total = terms_got[0, q // ranks, q % ranks].astype(jnp.float32)
         for g in range(1, groups):
-            total = total + terms_got[g, q].astype(jnp.float32)
+            total = total + terms_got[g, q // ranks, q % ranks].astype(jnp.float32)
         out[:, q * columns:(q + 1) * columns] = total.astype(jnp.bfloat16)
-    lax.fori_loop(0, patches * groups, end_terms, 0)
+
+    def end_fresh(i, carry):
+        finish_send(*fresh_args(i))
+        return carry
+
+    def end_weight(i, carry):
+        finish_send(*weight_args(i))
+        return carry
+
+    lax.fori_loop(0, heads, end_fresh, 0)
+    lax.fori_loop(0, ranks - 1, end_weight, 0)
+    for i in range(local):
+        finish_send(*seen_args(i))
+
+        def end_pass(k, carry):
+            finish_send(*pass_args(i, k))
+            return carry
+
+        def end_attended(k, carry):
+            finish_send(*attended_args(i, lax.rem(i + u, local), k))
+            return carry
+
+        def end_terms(k, carry):
+            finish_send(*terms_args(i, k))
+            return carry
+
+        lax.fori_loop(0, ranks - 1, end_pass, 0)
+        lax.fori_loop(0, local, end_attended, 0)
+        lax.fori_loop(0, groups, end_terms, 0)
 
 
 def solution(mesh):
@@ -240,6 +282,7 @@
         span = rows * groups
         heads = width // HEAD_DIM
         local = heads // groups
+        ranks = patches // local
         depth, columns = out_weight.shape
         bf16, f32 = jnp.bfloat16, jnp.float32
         vmem = pl.BlockSpec(memory_space=pltpu.VMEM)
@@ -254,19 +297,20 @@
                 pltpu.VMEM((3, rows, width), bf16),
                 pltpu.VMEM((2, span, depth), bf16),
                 pltpu.VMEM((2, span, depth), jnp.int32),
-                pltpu.VMEM((depth, columns), bf16),
+                pltpu.VMEM((ranks, depth, columns), bf16),
                 pltpu.VMEM((heads, 3, rows, HEAD_DIM), bf16),
                 pltpu.VMEM((local, groups, 3, rows, HEAD_DIM), bf16),
                 pltpu.VMEM((local, 2, span, HEAD_DIM), bf16),
-                pltpu.VMEM((patches, 2, span, HEAD_DIM), bf16),
+                pltpu.VMEM((ranks, local, 2, span, HEAD_DIM), bf16),
                 pltpu.VMEM((local, patches * span, HEAD_DIM), bf16),
                 pltpu.VMEM((local, patches * span, HEAD_DIM), bf16),
                 pltpu.VMEM((local, span, HEAD_DIM), bf16),
-                pltpu.VMEM((patches, local, span, HEAD_DIM), bf16),
-                pltpu.VMEM((patches, groups, rows, columns), bf16),
-                pltpu.VMEM((groups, patches, rows, columns), bf16),
-                dma((8,)), dma((heads,)), dma, dma((patches,)), dma,
-                dma((local, patches)), dma((patches,)), dma((patches, groups)), dma,
+                pltpu.VMEM((local, local, span, HEAD_DIM), bf16),
+                pltpu.VMEM((local, groups, ranks, rows, columns), bf16),
+                pltpu.VMEM((groups, local, ranks, rows, columns), bf16),
+                dma((8,)), dma((ranks,)), dma((ranks,)), dma((heads,)), dma,
+                dma((local,)), dma((local,)), dma((local, ranks)), dma((ranks,)),
+                dma((local, local)), dma((local,)), dma((local, groups)), dma,
             ],
             compiler_params=pltpu.CompilerParams(
                 collective_id=0, has_side_effects=True, vmem_limit_bytes=60 * 1024 * 1024

time: 32.7 us -> 30.8 us (0.942)
  Pallas kernels: 31 us -> 29 us
    pallas_call x1, Pallas kernels: 31 us -> 29 us  [on_device(): pl.pallas_call(functools.partial(kernel, patches, groups), out_shape=jax....]
where the time goes in v3:
time: 30.8 us; the launch traced here: 30.5 us
  Pallas kernels  29 us (94%)
  local copies, waits for them, and re-layouts  1.54 us (5%)
    pallas_call x1, Pallas kernels, on_device(): pl.pallas_call(functools.partial(kernel, patches, groups), out_shape=jax....  29 us
    unnamed x1, local copies, waits for them, and re-layouts  1.54 us

profile of v3, /device:TPU:1, one launch (start us, length us, event | category | flops | bytes accessed | tf_op | source)
XLA Modules:
  0.0 30.5 jit_solution(13155314294391672054)
XLA Ops:
  0.0 29.0 %shard_map.100 = bf16[16,3072]{1,0:T(8,128)(2,1)} custom-call(bf16[4,8]{1,0:T(4,128)(2,1)} %bitcast.2, bf16[4,8]{1,0:T(4,128)(2,1)} %bitcast.3, bf16[16,2048]{1,0:T(8,128)(2,1)} %fresh_q.1, bf16[16,2048]{1,0:T(8,128)(2,1)} %fresh_k.1, bf16[16,2048]{1,0:T(8,128)(2,1)} %fresh_v.1, bf16[512,512]{1,0:T(8,128)(2,1)} %old_k.1, bf16[512,512]{1,0:T(8,128)(2,1)} %old_v.1, ...), custom_call_target="tpu_custom_call" | custom-call | tf_op jit(solution)/shard_map/pallas_call | solution.py:291
  29.0 1.5 %copy.12 = bf16[16,3072]{1,0:T(8,128)(2,1)} copy(bf16[16,3072]{1,0:T(8,128)(2,1)} %shard_map.100) | data formatting | bytes 196608

commit v4 on v3

--- a/solution.py
+++ b/solution.py
@@ -45,10 +45,10 @@
     patches, groups,
     key_scales, value_scales,
     fresh_q, fresh_k, fresh_v, old_k, old_v, codes_k, codes_v, weight,
-    out,
+    terms_got,
     fresh_in, old_in, codes_in, weight_got,
     fresh_out, fresh_got, seen_out, seen_got, key_work, value_work,
-    attended_out, attended_got, terms_out, terms_got,
+    attended_out, attended_got, terms_out,
     load_sem, weight_send, weight_recv, fresh_send, fresh_recv,
     seen_send, seen_recv, pass_send, pass_recv,
     attended_send, attended_recv, terms_send, terms_recv,
@@ -64,6 +64,20 @@
     my_head = p // ranks
     my_rank = lax.rem(p, ranks)
 
+    barrier = pltpu.get_barrier_semaphore()
+    devices = patches * groups
+
+    def greet(i, carry):
+        to_p, to_u = i // groups, lax.rem(i, groups)
+
+        @pl.when(jnp.logical_not(jnp.logical_and(to_p == p, to_u == u)))
+        def _():
+            pl.semaphore_signal(barrier, inc=1, device_id=(to_p, to_u), device_id_type=MESH)
+
+        return carry
+
+    lax.fori_loop(0, devices, greet, 0)
+
     loads = [
         pltpu.make_async_copy(source, fresh_in.at[i], load_sem.at[i])
         for i, source in enumerate((fresh_q, fresh_k, fresh_v))
@@ -76,20 +90,6 @@
     loads.append(pltpu.make_async_copy(weight, weight_got.at[my_rank], load_sem.at[7]))
     for load in loads:
         load.start()
-
-    barrier = pltpu.get_barrier_semaphore()
-    devices = patches * groups
-
-    def greet(i, carry):
-        to_p, to_u = i // groups, lax.rem(i, groups)
-
-        @pl.when(jnp.logical_not(jnp.logical_and(to_p == p, to_u == u)))
-        def _():
-            pl.semaphore_signal(barrier, inc=1, device_id=(to_p, to_u), device_id_type=MESH)
-
-        return carry
-
-    lax.fori_loop(0, devices, greet, 0)
 
     for load in loads[:3]:
         load.wait()
@@ -201,9 +201,13 @@
 
         lax.fori_loop(0, local, start, 0)
 
+    columns = weight.shape[1]
+    width = ranks * columns
+    place = 0 if local == 1 else pl.multiple_of(my_head * width, width)
+
     def terms_args(index, i):
         to = lax.rem(u + 1 + i, groups)
-        return (terms_out.at[index, to], terms_got.at[u, my_head], terms_send.at[index, to],
+        return (terms_out.at[index, to], terms_got.at[u, :, pl.ds(place, width)], terms_send.at[index, to],
                 terms_recv, (my_rank * local + index, to), here)
 
     def project(slot):
@@ -212,7 +216,9 @@
         gathered = jnp.concatenate([attended_got[index, l] for l in range(local)], axis=1)
         for r in range(ranks):
             terms = jnp.dot(gathered, weight_got[r], preferred_element_type=jnp.float32)
-            terms_out[index, :, r] = terms.astype(jnp.bfloat16).reshape(groups, rows, terms.shape[1])
+            terms_out[index, :, :, r * columns:(r + 1) * columns] = terms.astype(jnp.bfloat16).reshape(
+                groups, rows, columns
+            )
 
         def start(i, carry):
             send(*terms_args(index, i))
@@ -234,12 +240,6 @@
         project(slot)
 
     wait_bytes(terms_got, terms_recv)
-    columns = weight.shape[1]
-    for q in range(patches):
-        total = terms_got[0, q // ranks, q % ranks].astype(jnp.float32)
-        for g in range(1, groups):
-            total = total + terms_got[g, q // ranks, q % ranks].astype(jnp.float32)
-        out[:, q * columns:(q + 1) * columns] = total.astype(jnp.bfloat16)
 
     def end_fresh(i, carry):
         finish_send(*fresh_args(i))
@@ -288,11 +288,11 @@
         vmem = pl.BlockSpec(memory_space=pltpu.VMEM)
         hbm = pl.BlockSpec(memory_space=pltpu.HBM)
         dma = pltpu.SemaphoreType.DMA
-        return pl.pallas_call(
+        terms = pl.pallas_call(
             functools.partial(kernel, patches, groups),
-            out_shape=jax.ShapeDtypeStruct((rows, patches * columns), bf16),
+            out_shape=jax.ShapeDtypeStruct((groups, rows, patches * columns), bf16),
             in_specs=[vmem] * 2 + [hbm] * 8,
-            out_specs=vmem,
+            out_specs=hbm,
             scratch_shapes=[
                 pltpu.VMEM((3, rows, width), bf16),
                 pltpu.VMEM((2, span, depth), bf16),
@@ -306,8 +306,7 @@
                 pltpu.VMEM((local, patches * span, HEAD_DIM), bf16),
                 pltpu.VMEM((local, span, HEAD_DIM), bf16),
                 pltpu.VMEM((local, local, span, HEAD_DIM), bf16),
-                pltpu.VMEM((local, groups, ranks, rows, columns), bf16),
-                pltpu.VMEM((groups, local, ranks, rows, columns), bf16),
+                pltpu.VMEM((local, groups, rows, ranks * columns), bf16),
                 dma((8,)), dma((ranks,)), dma((ranks,)), dma((heads,)), dma,
                 dma((local,)), dma((local,)), dma((local, ranks)), dma((ranks,)),
                 dma((local, local)), dma((local,)), dma((local, groups)), dma,
@@ -319,6 +318,10 @@
             key_code_scales.T, value_scales.T, fresh_queries, fresh_keys, fresh_values,
             outdated_keys, stale_values, key_codes, value_codes, out_weight,
         )
+        total = terms[0].astype(f32)
+        for g in range(1, groups):
+            total = total + terms[g].astype(f32)
+        return total.astype(bf16)
 
     return jax.shard_map(
         on_device,

time: 30.8 us -> 30.1 us (0.977)
  other arithmetic: 0 us -> 1.73 us
  local copies, waits for them, and re-layouts: 1.54 us -> 0 us
  Pallas kernels: 29 us -> 28.2 us
    add x0 -> x1, other arithmetic: none -> 1.73 us  [on_device(): total = total + terms[g].astype(f32)]
    unnamed x1 -> x0, local copies, waits for them, and re-layouts: 1.54 us -> none
    pallas_call x1, Pallas kernels: 29 us -> 28.2 us  [on_device(): pl.pallas_call(functools.partial(kernel, patches, groups), out_shape=jax....]
where the time goes in v4:
time: 30.1 us; the launch traced here: 29.9 us
  Pallas kernels  28.2 us (94%)
  other arithmetic  1.73 us (6%)
    pallas_call x1, Pallas kernels, on_device(): pl.pallas_call(functools.partial(kernel, patches, groups), out_shape=jax....  28.2 us
    add x1, other arithmetic, on_device(): total = total + terms[g].astype(f32)  1.73 us

profile of v4, /device:TPU:1, one launch (start us, length us, event | category | flops | bytes accessed | tf_op | source)
XLA Modules:
  0.0 29.9 jit_solution(4722903740233200625)
XLA Ops:
  0.0 28.2 %shard_map.100 = bf16[4,16,3072]{2,1,0:T(8,128)(2,1)} custom-call(bf16[4,8]{1,0:T(4,128)(2,1)} %bitcast.4, bf16[4,8]{1,0:T(4,128)(2,1)} %bitcast.5, bf16[16,2048]{1,0:T(8,128)(2,1)} %fresh_q.1, bf16[16,2048]{1,0:T(8,128)(2,1)} %fresh_k.1, bf16[16,2048]{1,0:T(8,128)(2,1)} %fresh_v.1, bf16[512,512]{1,0:T(8,128)(2,1)} %old_k.1, bf16[512,512]{1,0:T(8,128)(2,1)} %old_v.1, ...), custom_call_target="tpu_custom_call" | custom-call | tf_op jit(solution)/shard_map/pallas_call | solution.py:291
  28.2 1.7 %fusion = bf16[16,3072]{1,0:T(8,128)(2,1)} fusion(bf16[4,16,3072]{2,1,0:T(8,128)(2,1)} %shard_map.100), kind=kLoop, calls=%fused_computation.1 | loop fusion | flops 393216 | bytes 491520 | tf_op jit(solution)/shard_map/add | solution.py:323

commit v5 on v4

--- a/solution.py
+++ b/solution.py
@@ -177,7 +177,7 @@
                 attended_send.at[slot, m], attended_recv.at[index], (m * ranks + my_rank, u), here)
 
     def attend(slot):
-        index = lax.rem(slot + u, local)
+        index = lax.rem(slot, local)
         patch = my_rank * local + index
         query = fresh_got[index, :, 0].reshape(span, HEAD_DIM)
         place = lax.rem(patch, ranks) * local + patch // ranks
@@ -211,7 +211,7 @@
                 terms_recv, (my_rank * local + index, to), here)
 
     def project(slot):
-        index = lax.rem(slot + u, local)
+        index = lax.rem(slot, local)
         wait_bytes(attended_got.at[index], attended_recv.at[index])
         gathered = jnp.concatenate([attended_got[index, l] for l in range(local)], axis=1)
         for r in range(ranks):
@@ -259,7 +259,7 @@
             return carry
 
         def end_attended(k, carry):
-            finish_send(*attended_args(i, lax.rem(i + u, local), k))
+            finish_send(*attended_args(i, lax.rem(i, local), k))
             return carry
 
         def end_terms(k, carry):

time: 30.1 us -> 28.9 us (0.960)
  the two profiles are of different devices: /device:TPU:1 before, /device:TPU:3 now
where the time goes in v5:
time: 28.9 us; the launch traced here: 28.8 us
  Pallas kernels  27 us (93%)
  other arithmetic  1.73 us (6%)
    pallas_call x1, Pallas kernels, on_device(): pl.pallas_call(functools.partial(kernel, patches, groups), out_shape=jax....  27 us
    add x1, other arithmetic, on_device(): total = total + terms[g].astype(f32)  1.73 us

profile of v5, /device:TPU:3, one launch (start us, length us, event | category | flops | bytes accessed | tf_op | source)
XLA Modules:
  0.0 28.8 jit_solution(7528550703215232269)
XLA Ops:
  0.0 27.0 %shard_map.100 = bf16[4,16,3072]{2,1,0:T(8,128)(2,1)} custom-call(bf16[4,8]{1,0:T(4,128)(2,1)} %bitcast.4, bf16[4,8]{1,0:T(4,128)(2,1)} %bitcast.5, bf16[16,2048]{1,0:T(8,128)(2,1)} %fresh_q.1, bf16[16,2048]{1,0:T(8,128)(2,1)} %fresh_k.1, bf16[16,2048]{1,0:T(8,128)(2,1)} %fresh_v.1, bf16[512,512]{1,0:T(8,128)(2,1)} %old_k.1, bf16[512,512]{1,0:T(8,128)(2,1)} %old_v.1, ...), custom_call_target="tpu_custom_call" | custom-call | tf_op jit(solution)/shard_map/pallas_call | solution.py:291
  27.0 1.7 %fusion = bf16[16,3072]{1,0:T(8,128)(2,1)} fusion(bf16[4,16,3072]{2,1,0:T(8,128)(2,1)} %shard_map.100), kind=kLoop, calls=%fused_computation.1 | loop fusion | flops 393216 | bytes 491520 | tf_op jit(solution)/shard_map/add | solution.py:323
